TPU v7x, 32 devices: a whole 2x2x4 slice. The times are simulated.
32 devices in a mesh: ens: 2 (over x), bin: 16 (over z, y, core).
Axes of the slice: x: 2, y: 2, z: 4, core: 2. Of those that a mesh axis runs over, the one named last changes fastest.
Arguments:
- spectrum: bfloat16 [1536, 16, 512], P(('ens', 'bin')), parts along dimension 0, may hold values from 0.049804688 to 2
- land_mask: int32 [16, 512], replicated, may hold values 0 or 1
- depth_class: int32 [16, 512], replicated, may hold values from 0 to 7
- upwind_signs: int32 [2, 768], replicated, may hold values from -1 to 1, as said below
- group_speed: float32 [8, 24], replicated, may hold values from 0.2 to 0.7
- speed_ratio: float32 [8, 24], replicated, may hold values from 0.5 to 1
- mixing: bfloat16 [768, 768], replicated, may hold values from -0.0546875 to 0.0546875
- growth: float32 [768], replicated, may hold values from 0.01 to 0.08
- wind_speed: float32 [32, 512], P('ens'), parts along dimension 0, may hold values from 0.5 to 2
- water_depth: float32 [8], replicated, may hold values from 1 to 4
- currents: float32 [4, 16, 512], P('ens', 'bin'), parts along dimension 0, may hold values from -6 to 6
Outputs:
- spectrum_next: bfloat16 [1536, 16, 512], P(('ens', 'bin')), parts along dimension 0
- currents_next: float32 [4, 16, 512], P('ens', 'bin'), parts along dimension 0
There are 2 independent parts, one for each index of `ens`. A program takes and returns all parts, laid end to end along the dimension named above; an argument that names none is the same for every part. Nothing has to cross between parts.
Inputs may be any that keep to these rules, and one draw needn't show every extreme that they name: `upwind_signs`: each entry is -1 or +1.
All inputs are finite; a program needn't handle non-finite values.
Results may differ from a plain program's by a relative error of at most 0.0052.
Values may be sent and summed in bfloat16 or wider, within the bound.
A program may use at most 64 MiB of HBM per device.

v0:
```python
import math

import jax
import jax.numpy as jnp
from jax import lax
from jax.sharding import PartitionSpec as P

NDIR = 32
NFREQ = 24
NCLASS = 8
SUBS = 8


STRESS_SCALE = 0.0625


def extended(shard, sides, width):
    for axis, dim in sides:
        peers, length = (lax.axis_size(axis), shard.shape[dim])
        up = [(i, (i + 1) % peers) for i in range(peers - 1)]
        down = [(j, i) for i, j in up]
        last = lax.slice_in_dim(shard, length - width, length, axis=dim)
        initial = lax.slice_in_dim(shard, 0, width, axis=dim)
        before = lax.ppermute(last, axis, up)
        after = lax.ppermute(initial, axis, down)
        shard = jnp.concatenate([before, shard, after], axis=dim)
    return shard


def angle_of(direction):
    return 2.0 * math.pi * (direction + 0.5) / NDIR


def from_lower(field, axis):
    width = [(0, 0)] * field.ndim
    width[axis] = (1, 0)
    padded = jnp.pad(field, width)
    return lax.slice_in_dim(padded, 0, field.shape[axis], axis=axis)


def from_upper(field, axis):
    width = [(0, 0)] * field.ndim
    width[axis] = (0, 1)
    padded = jnp.pad(field, width)
    return lax.slice_in_dim(padded, 1, field.shape[axis] + 1, axis=axis)


def upwind_step(energy, celerity, cos_abs, sin_abs, sign_x, sign_y, maskf):
    axis_x = energy.ndim - 2
    axis_y = energy.ndim - 1
    flux_x = maskf * (sign_x * celerity * cos_abs * energy)
    flux_y = maskf * (sign_y * celerity * sin_abs * energy)
    diff_x = jnp.where(
        sign_x > 0, flux_x - from_lower(flux_x, axis_x), from_upper(flux_x, axis_x) - flux_x
    )
    diff_y = jnp.where(
        sign_y > 0, flux_y - from_lower(flux_y, axis_y), from_upper(flux_y, axis_y) - flux_y
    )
    return maskf * (energy - diff_x - diff_y)


def integrate(energy, mixing, growth, wind_flat):
    for substep in range(SUBS):
        rounded = energy.astype(jnp.bfloat16)
        energy = (
            energy
            + jnp.dot(mixing, rounded, preferred_element_type=jnp.float32)
            + growth[:, None] * wind_flat[None, :] * energy
        )
    return energy.astype(jnp.bfloat16)


def radiation(fresh, ratio_map):
    energy = fresh.astype(jnp.float32).reshape(NDIR, NFREQ, -1)
    theta = angle_of(jnp.arange(NDIR, dtype=jnp.float32))
    cosine = jnp.cos(theta)
    sine = jnp.sin(theta)
    coeff = jnp.stack([cosine * cosine + 1.0, cosine * sine, sine * sine + 1.0])
    weighted = jnp.einsum("cd,dfn->cfn", coeff, energy, precision=lax.Precision.HIGHEST)
    total = jnp.sum(energy, axis=(0, 1))
    flat_ratio = ratio_map.reshape(NFREQ, -1)
    offset = jnp.array([0.5, 0.0, 0.5], dtype=jnp.float32)
    stress = (
        jnp.sum(flat_ratio[None] * weighted, axis=1) - offset[:, None] * total[None]
    ) * STRESS_SCALE
    return stress.reshape(3, fresh.shape[1], fresh.shape[2])


def forcing(stress_wide, currents, depth_map, maskf):
    slope_x = (stress_wide[:, 2:] - stress_wide[:, :-2]) * 0.5
    inner = stress_wide[:, 1:-1]
    padded_y = jnp.pad(inner, ((0, 0), (0, 0), (1, 1)))
    slope_y = (padded_y[:, :, 2:] - padded_y[:, :, :-2]) * 0.5
    force = jnp.stack([-(slope_x[0] + slope_y[1]), -(slope_x[1] + slope_y[2])])
    return maskf * (currents + force / depth_map)


def local(
    spectrum,
    land_mask,
    depth_class,
    upwind_signs,
    group_speed,
    speed_ratio,
    mixing,
    growth,
    wind_speed,
    water_depth,
    currents,
):
    bin_local = spectrum.shape[0]
    own_rows = currents.shape[1]
    device_index = lax.axis_index("bin")
    bin_ids = device_index * bin_local + jnp.arange(bin_local, dtype=jnp.int32)
    theta = angle_of((bin_ids // NFREQ).astype(jnp.float32))
    cos_abs = jnp.abs(jnp.cos(theta))[:, None, None]
    sin_abs = jnp.abs(jnp.sin(theta))[:, None, None]
    freq_select = (
        (bin_ids % NFREQ)[:, None] == jnp.arange(NFREQ, dtype=jnp.int32)[None, :]
    ).astype(jnp.float32)
    speed_table = jnp.dot(group_speed, freq_select.T, precision=lax.Precision.HIGHEST)
    classes = (depth_class[None] == jnp.arange(NCLASS, dtype=jnp.int32)[:, None, None]).astype(
        jnp.float32
    )
    celerity = jnp.einsum("kb,kxy->bxy", speed_table, classes, precision=lax.Precision.HIGHEST)
    upwind = lax.dynamic_slice_in_dim(upwind_signs, device_index * bin_local, bin_local, 1).astype(
        jnp.float32
    )
    maskf = land_mask.astype(jnp.float32)
    moved = upwind_step(
        spectrum.astype(jnp.float32),
        celerity,
        cos_abs,
        sin_abs,
        upwind[0][:, None, None],
        upwind[1][:, None, None],
        maskf,
    ).astype(jnp.bfloat16)
    first_row = device_index * own_rows
    wind_rows = lax.dynamic_slice_in_dim(wind_speed, first_row, own_rows, 0)
    class_rows = lax.dynamic_slice_in_dim(depth_class, first_row, own_rows, 0)
    mask_own = lax.dynamic_slice_in_dim(maskf, first_row, own_rows, 0)
    ratio_classes = (class_rows[None] == jnp.arange(NCLASS, dtype=jnp.int32)[:, None, None]).astype(
        jnp.float32
    )
    ratio_map = jnp.einsum(
        "kf,kxy->fxy", speed_ratio, ratio_classes, precision=lax.Precision.HIGHEST
    )

    def owner_step(received, wind_block):
        energy = received.astype(jnp.float32).reshape(received.shape[0], -1)
        return integrate(energy, mixing, growth, wind_block.reshape(-1)).reshape(received.shape)

    pieces = [(lax.all_to_all(moved, "bin", split_axis=1, concat_axis=0, tiled=True), wind_rows)]
    fresh = jnp.concatenate([owner_step(piece, wind_part) for piece, wind_part in pieces], axis=2)
    stress = extended(radiation(fresh, ratio_map), (("bin", 1),), 1)
    spectrum_next = lax.all_to_all(fresh, "bin", split_axis=0, concat_axis=1, tiled=True)
    depth_map = jnp.einsum("k,kxy->xy", water_depth, ratio_classes, precision=lax.Precision.HIGHEST)
    return (spectrum_next, forcing(stress, currents, depth_map, mask_own))


def solution(mesh):
    in_specs = (
        P(("ens", "bin"), None, None),
        P(),
        P(),
        P(),
        P(),
        P(),
        P(),
        P(),
        P("ens", None),
        P(),
        P("ens", "bin", None),
    )
    out_specs = (P(("ens", "bin"), None, None), P("ens", "bin", None))
    return jax.shard_map(local, mesh=mesh, in_specs=in_specs, out_specs=out_specs, check_vma=False)
```

profile of v0, /device:TPU:15, one launch (start us, length us, event | category | flops | bytes accessed | tf_op | source)
XLA Modules:
  0.0 73.2 jit_solution(14137657411433018170)
XLA Ops:
  0.6 0.0 copy-start
  0.7 0.1 sine_abs_fusion
  0.7 0.8 %dynamic-slice_convert_fusion = f32[2,48]{1,0:T(2,128)S(1)} fusion(s32[2,768]{1,0:T(2,128)} %param.15, s32[]{:T(128)S(6)} %select_n.38), kind=kLoop, calls=%fused_computation.81 | loop fusion | flops 96 | bytes 772 | tf_op jit(solution)/shard_map/convert_element_type | solution.py:126
  1.6 0.8 %convert_element_type.70 = f32[16,512]{1,0:T(8,128)S(1)} convert(s32[16,512]{1,0:T(8,128)} %param.13) | non-fusion elementwise | flops 8192 | bytes 65536 | tf_op jit(solution)/shard_map/convert_element_type | solution.py:129
  2.3 0.9 %convolution_bitcast_fusion.1 = f32[48,8,1]{0,1,2:T(8,128)S(1)} fusion(f32[8,24]{1,0:T(8,128)} %param.16, s32[48]{0:T(128)S(1)} %and_select_fusion.1), kind=kOutput, calls=%fused_computation.47 | convolution fusion | flops 111744 | bytes 2496 | tf_op jit(solution)/shard_map/dot_general | solution.py:121
  3.2 3.0 %fusion.10 = (f32[48,16,512]{2,0,1:T(8,128)S(1)}, f32[48,16,512]{2,0,1:T(8,128)S(1)}) fusion(f32[48]{0:T(128)S(1)} %get-tuple-element.17, f32[48]{0:T(128)S(1)} %get-tuple-element.12, f32[16,512]{1,0:T(8,128)S(1)} %convert_element_type.70, bf16[48,16,512]{2,1,0:T(8,128)(2,1)} %param.12, f32[48]{0:T(128)S(1)} %get-tuple-element.16, ...), kind=kOutput, calls=%fused_computation.26 | convolution fusion | flops 41353216 | bytes 4000000 | tf_op jit(solution)/shard_map/kb,kxy->bxy/dot_general | solution.py:125
  6.2 0.0 copy-done.1
  6.2 2.1 %fusion.7 = bf16[48,16,512]{2,0,1:T(8,128)(2,1)} fusion(f32[48,16,512]{2,0,1:T(8,128)S(1)} %get-tuple-element.7, f32[48,16,512]{2,0,1:T(8,128)S(1)} %get-tuple-element.6, f32[16,512]{1,0:T(8,128)S(1)} %convert_element_type.70, pred[48]{0:T(512)(128)(4,1)S(1)} %get-tuple-element.11, pred[48]{0:T(512)(128)(4,1)S(1)} %get-tuple-element.10, ...), kind=kLoop, calls=%fused_computation.23 | loop fusion | flops 4325376 | bytes 4751456 | tf_op jit(solution)/shard_map/convert_element_type | solution.py:138
  8.3 6.7 %all-to-all-start = ((bf16[48,16,512]{2,0,1:T(8,128)(2,1)}), bf16[48,16,512]{2,0,1:T(8,128)(2,1)S(1)}, u32[]{:S(2)}, u32[]{:S(2)}) async-start(bf16[48,16,512]{2,0,1:T(8,128)(2,1)} %fusion.7), calls=%async_computation | async-start | bytes 1572864 | tf_op jit(solution)/shard_map/all_to_all | solution.py:154
  15.0 0.6 multiply_add_fusion
  15.7 0.7 constant_dynamic-slice_fusion
  16.4 0.7 constant_dynamic-slice_fusion.2
  17.1 0.0 copy-done.5
  17.1 0.7 fusion.31
  17.8 16.4 %all-to-all-done = bf16[48,16,512]{2,0,1:T(8,128)(2,1)S(1)} async-done(((bf16[48,16,512]{2,0,1:T(8,128)(2,1)}), bf16[48,16,512]{2,0,1:T(8,128)(2,1)S(1)}, u32[]{:S(2)}, u32[]{:S(2)}) %all-to-all-start) | async-done | bytes 786464 | tf_op jit(solution)/shard_map/all_to_all | solution.py:154
  34.3 0.3 copy.25
  34.5 0.0 copy-done
  34.6 0.0 copy-done.3
  34.6 1.0 %fusion.9 = f32[768,512]{0,1:T(8,128)S(1)} fusion(bf16[768,512]{0,1:T(8,128)(2,1)S(1)} %copy.25, bf16[768,512]{1,0:T(8,128)(2,1)S(1)} %bitcast.77, bf16[768,768]{1,0:T(8,128)(2,1)S(1)} %copy-done, f32[512]{0:T(512)S(1)} %bitcast.84, f32[768]{0:T(1024)S(1)} %copy-done.3), kind=kOutput, calls=%fused_computation.25 | convolution fusion | flops 605945856 | bytes 4330496 | tf_op jit(solution)/shard_map/dot_general | solution.py:67
  35.6 0.8 %fusion.12 = f32[768,512]{0,1:T(8,128)S(1)} fusion(f32[768,512]{0,1:T(8,128)S(1)} %fusion.9, bf16[768,768]{1,0:T(8,128)(2,1)S(1)} %copy-done, f32[512]{0:T(512)S(1)} %bitcast.85, f32[768]{0:T(1024)S(1)} %copy-done.3), kind=kOutput, calls=%fused_computation.28 | convolution fusion | flops 605945856 | bytes 4330496 | tf_op jit(solution)/shard_map/dot_general | solution.py:67
  36.4 0.8 %fusion.13 = f32[768,512]{0,1:T(8,128)S(1)} fusion(f32[768,512]{0,1:T(8,128)S(1)} %fusion.12, bf16[768,768]{1,0:T(8,128)(2,1)S(1)} %copy-done, f32[512]{0:T(512)S(1)} %bitcast.86, f32[768]{0:T(1024)S(1)} %copy-done.3), kind=kOutput, calls=%fused_computation.29 | convolution fusion | flops 605945856 | bytes 4330496 | tf_op jit(solution)/shard_map/dot_general | solution.py:67
  37.3 0.8 %fusion.14 = f32[768,512]{0,1:T(8,128)S(1)} fusion(f32[768,512]{0,1:T(8,128)S(1)} %fusion.13, bf16[768,768]{1,0:T(8,128)(2,1)S(1)} %copy-done, f32[512]{0:T(512)S(1)} %bitcast.87, f32[768]{0:T(1024)S(1)} %copy-done.3), kind=kOutput, calls=%fused_computation.30 | convolution fusion | flops 605945856 | bytes 4330496 | tf_op jit(solution)/shard_map/dot_general | solution.py:67
  38.1 0.8 %fusion.15 = f32[768,512]{0,1:T(8,128)S(1)} fusion(f32[768,512]{0,1:T(8,128)S(1)} %fusion.14, bf16[768,768]{1,0:T(8,128)(2,1)S(1)} %copy-done, f32[512]{0:T(512)S(1)} %bitcast.88, f32[768]{0:T(1024)S(1)} %copy-done.3), kind=kOutput, calls=%fused_computation.31 | convolution fusion | flops 605945856 | bytes 4330496 | tf_op jit(solution)/shard_map/dot_general | solution.py:67
  39.0 0.8 %fusion.16 = f32[768,512]{0,1:T(8,128)S(1)} fusion(f32[768,512]{0,1:T(8,128)S(1)} %fusion.15, bf16[768,768]{1,0:T(8,128)(2,1)S(1)} %copy-done, f32[512]{0:T(512)S(1)} %bitcast.89, f32[768]{0:T(1024)S(1)} %copy-done.3), kind=kOutput, calls=%fused_computation.32 | convolution fusion | flops 605945856 | bytes 4330496 | tf_op jit(solution)/shard_map/dot_general | solution.py:67
  39.9 0.9 %fusion.17 = f32[768,512]{0,1:T(8,128)S(1)} fusion(f32[768,512]{0,1:T(8,128)S(1)} %fusion.16, bf16[768,768]{1,0:T(8,128)(2,1)S(1)} %copy-done, f32[512]{0:T(512)S(1)} %bitcast.90, f32[768]{0:T(1024)S(1)} %copy-done.3), kind=kOutput, calls=%fused_computation.33 | convolution fusion | flops 605945856 | bytes 4330496 | tf_op jit(solution)/shard_map/dot_general | solution.py:67
  40.7 1.0 %convert_reduce_fusion = (f32[512]{0:T(512)S(1)}, bf16[768,512]{0,1:T(8,128)(2,1)S(1)}) fusion(f32[768,512]{0,1:T(8,128)S(1)} %fusion.17, f32[512]{0:T(512)S(1)} %bitcast.91, f32[768]{0:T(1024)S(1)} %copy-done.3, bf16[768,768]{1,0:T(8,128)(2,1)S(1)} %copy-done), kind=kOutput, calls=%fused_computation.43 | convolution fusion | flops 607124992 | bytes 3546112 | tf_op jit(solution)/shard_map/dot_general | solution.py:67
  41.7 0.5 broadcast.229
  42.2 1.2 %reduce.2 = bf16[768,512]{0,1:T(8,128)(2,1)S(1)} reduce(bf16[768,1,512]{0,2,1:T(8,128)(2,1)S(1)} %bitcast.78, bf16[]{:T(256)} %broadcast.229), dimensions={1}, to_apply=%copy.26.reduce_sub_computation | reduce | bytes 1572866 | tf_op jit(solution)/shard_map/reshape | solution.py:152
  43.5 0.3 copy.36
  43.7 1.4 %reshape.242 = bf16[16,2,12288]{2,1,0:T(2,128)(2,1)} reshape(bf16[768,512]{1,0:T(8,128)(2,1)S(1)} %copy.36) | data formatting | bytes 1572864
  45.2 5.1 %all-to-all-start.1 = ((bf16[16,2,12288]{2,1,0:T(2,128)(2,1)}), bf16[16,2,12288]{2,1,0:T(2,128)(2,1)S(1)}, u32[]{:S(2)}, u32[]{:S(2)}) async-start(bf16[16,2,12288]{2,1,0:T(2,128)(2,1)} %reshape.242), calls=%async_computation.1 | async-start | bytes 1572864 | tf_op jit(solution)/shard_map/all_to_all | solution.py:157
  50.3 0.6 fusion.46
  50.9 0.0 copy-done.4
  50.9 0.8 %convolution_bitcast_fusion = f32[24,512]{1,0:T(8,128)} fusion(f32[8,24]{1,0:T(8,128)S(1)} %copy-done.4, s32[512]{0:T(512)S(1)} %bitcast.83), kind=kOutput, calls=%fused_computation.46 | convolution fusion | flops 1183744 | bytes 51968 | tf_op jit(solution)/shard_map/kf,kxy->fxy/dot_general | solution.py:146
  51.7 0.3 copy.27
  52.0 0.4 copy-done.6
  52.3 1.4 %fusion.20 = f32[3,512]{1,0:T(4,128)S(1)} fusion(bf16[32,24,512]{2,1,0:T(8,128)(2,1)S(1)} %bitcast.80, f32[24,512]{1,0:T(8,128)} %convolution_bitcast_fusion, f32[1,32]{1,0:T(1,128)} %get-tuple-element.18, f32[1,32]{1,0:T(1,128)S(1)} %copy-done.6, f32[1,32]{1,0:T(1,128)} %get-tuple-element.19), kind=kOutput, calls=%fused_computation.45 | convolution fusion | flops 14228160 | bytes 842112 | tf_op jit(solution)/shard_map/cd,dfn->cfn/dot_general | solution.py:79
  53.7 0.7 %subtract_multiply_fusion.2 = f32[3,1,512]{2,1,0:T(1,128)S(1)} fusion(f32[3,512]{1,0:T(4,128)S(1)} %fusion.20, f32[512]{0:T(512)S(1)} %get-tuple-element.14, f32[3]{0:T(128)} %constant.54.clone), kind=kLoop, calls=%fused_computation.67 | loop fusion | flops 4608 | bytes 14348 | tf_op jit(solution)/shard_map/mul | solution.py:83
  54.5 2.3 %collective-permute-start = (f32[3,1,512]{2,1,0:T(1,128)S(1)}, f32[3,1,512]{2,1,0:T(1,128)S(1)}, u32[]{:S(2)}, u32[]{:S(2)}) collective-permute-start(f32[3,1,512]{2,1,0:T(1,128)S(1)} %subtract_multiply_fusion.2), channel_id=1, source_target_pairs={{1,0},{2,1},{3,2},{4,3},{5,4},{6,5},{7,6},{8,7},{9,8},{10,9},{11,1... | collective-permute-start | bytes 18440 | tf_op jit(solution)/shard_map/ppermute | solution.py:25
  56.7 4.2 %collective-permute-start.1 = (f32[3,1,512]{2,1,0:T(1,128)S(1)}, f32[3,1,512]{2,1,0:T(1,128)S(1)}, u32[]{:S(2)}, u32[]{:S(2)}) collective-permute-start(f32[3,1,512]{2,1,0:T(1,128)S(1)} %subtract_multiply_fusion.2), channel_id=1, source_target_pairs={{0,1},{1,2},{2,3},{3,4},{4,5},{5,6},{6,7},{7,8},{8,9},{9,10},{10,1... | collective-permute-start | bytes 18440 | tf_op jit(solution)/shard_map/ppermute | solution.py:24
  60.9 0.1 subtract_multiply_fusion
  61.0 8.6 %collective-permute-done = f32[3,1,512]{2,1,0:T(1,128)S(1)} collective-permute-done((f32[3,1,512]{2,1,0:T(1,128)S(1)}, f32[3,1,512]{2,1,0:T(1,128)S(1)}, u32[]{:S(2)}, u32[]{:S(2)}) %collective-permute-start) | collective-permute-done | bytes 6176 | tf_op jit(solution)/shard_map/ppermute | solution.py:25
  69.6 0.0 collective-permute-done.1
  69.6 1.3 %fusion.35 = f32[2,1,512]{2,1,0:T(1,128)} fusion(f32[2,1,512]{2,1,0:T(1,128)S(1)} %copy-done.2, f32[1,1,512]{2,1,0:T(1,128)S(1)} %get-tuple-element.9, f32[1,1,512]{2,1,0:T(1,128)S(1)} %get-tuple-element.8, f32[512]{0:T(512)} %bitcast.92, f32[512]{0:T(512)S(1)} %bitcast.81), kind=kLoop, calls=%fused_computation.69 | loop fusion | flops 4096 | bytes 16384 | tf_op jit(solution)/shard_map/mul | solution.py:95
  70.9 0.0 all-to-all-done.1
  70.9 0.7 %reshape.243 = bf16[768,1,512]{2,1,0:T(2,128)(2,1)S(1)} reshape(bf16[16,2,12288]{2,1,0:T(2,128)(2,1)S(1)} %all-to-all-done.1) | data formatting | bytes 1572864
  71.7 0.2 copy.30
  71.9 1.3 %copy.29 = bf16[48,16,512]{2,1,0:T(8,128)(2,1)} copy(bf16[48,16,512]{2,0,1:T(8,128)(2,1)S(1)} %bitcast.79) | data formatting | bytes 1572864
  (13 shorter events, 0.1 us)
Async XLA Ops:
  0.6 33.9 %copy-start = (bf16[768,768]{1,0:T(8,128)(2,1)S(1)}, bf16[768,768]{1,0:T(8,128)(2,1)}, u32[]{:S(2)}) copy-start(bf16[768,768]{1,0:T(8,128)(2,1)} %param.18) | copy-start | bytes 3538948
  3.2 3.0 %copy-start.1 = (bf16[48,16,512]{2,1,0:T(8,128)(2,1)S(1)}, bf16[48,16,512]{2,1,0:T(8,128)(2,1)}, u32[]{:S(2)}) copy-start(bf16[48,16,512]{2,1,0:T(8,128)(2,1)} %param.12) | copy-start | bytes 2359300
  8.3 8.8 %copy-start.5 = (f32[8]{0:T(128)S(1)}, f32[8]{0:T(128)}, u32[]{:S(2)}) copy-start(f32[8]{0:T(128)} %param.21) | copy-start | bytes 100
  8.3 26.2 %copy-start.3 = (f32[768]{0:T(1024)S(1)}, f32[768]{0:T(1024)}, u32[]{:S(2)}) copy-start(f32[768]{0:T(1024)} %param.19) | copy-start | bytes 9220
  8.3 25.9 %all-to-all-start = ((bf16[48,16,512]{2,0,1:T(8,128)(2,1)}), bf16[48,16,512]{2,0,1:T(8,128)(2,1)S(1)}, u32[]{:S(2)}, u32[]{:S(2)}) async-start(bf16[48,16,512]{2,0,1:T(8,128)(2,1)} %fusion.7), calls=%async_computation | async-start | bytes 1572864 | tf_op jit(solution)/shard_map/all_to_all | solution.py:154
  45.2 5.7 %copy-start.4 = (f32[8,24]{1,0:T(8,128)S(1)}, f32[8,24]{1,0:T(8,128)}, u32[]{:S(2)}) copy-start(f32[8,24]{1,0:T(8,128)} %param.17) | copy-start | bytes 2308
  45.2 25.7 %all-to-all-start.1 = ((bf16[16,2,12288]{2,1,0:T(2,128)(2,1)}), bf16[16,2,12288]{2,1,0:T(2,128)(2,1)S(1)}, u32[]{:S(2)}, u32[]{:S(2)}) async-start(bf16[16,2,12288]{2,1,0:T(2,128)(2,1)} %reshape.242), calls=%async_computation.1 | async-start | bytes 1572864 | tf_op jit(solution)/shard_map/all_to_all | solution.py:157
  50.3 19.3 %copy-start.2 = (f32[2,1,512]{2,1,0:T(1,128)S(1)}, f32[2,1,512]{2,1,0:T(1,128)}, u32[]{:S(2)}) copy-start(f32[2,1,512]{2,1,0:T(1,128)} %param.22) | copy-start | bytes 12292
  51.7 0.7 copy-start.6
  54.5 15.1 %collective-permute-start = (f32[3,1,512]{2,1,0:T(1,128)S(1)}, f32[3,1,512]{2,1,0:T(1,128)S(1)}, u32[]{:S(2)}, u32[]{:S(2)}) collective-permute-start(f32[3,1,512]{2,1,0:T(1,128)S(1)} %subtract_multiply_fusion.2), channel_id=1, source_target_pairs={{1,0},{2,1},{3,2},{4,3},{5,4},{6,5},{7,6},{8,7},{9,8},{10,9},{11,1... | collective-permute-start | bytes 18440 | tf_op jit(solution)/shard_map/ppermute | solution.py:25
  56.7 12.9 %collective-permute-start.1 = (f32[3,1,512]{2,1,0:T(1,128)S(1)}, f32[3,1,512]{2,1,0:T(1,128)S(1)}, u32[]{:S(2)}, u32[]{:S(2)}) collective-permute-start(f32[3,1,512]{2,1,0:T(1,128)S(1)} %subtract_multiply_fusion.2), channel_id=1, source_target_pairs={{0,1},{1,2},{2,3},{3,4},{4,5},{5,6},{6,7},{7,8},{8,9},{9,10},{10,1... | collective-permute-start | bytes 18440 | tf_op jit(solution)/shard_map/ppermute | solution.py:24
where the time goes:
time: 73.9 us; the launch traced here: 73.2 us
  waiting for transfers between devices  25 us (34%)
  starting transfers between devices  18.2 us (25%)
  matrix products  13.9 us (19%)
  other arithmetic  8.33 us (11%)
  local copies, waits for them, and re-layouts  6.93 us (9%)
  between operations  0.84 us (1%)
    all_to_all x1, waiting for transfers between devices, local(): lax.all_to_all(moved, 'bin', split_axis=1, concat_axis=0, tiled=True)  16.4 us
    ppermute x1, waiting for transfers between devices, extended(): after = lax.ppermute(initial, axis, down)  8.56 us
    dot_general x8, matrix products, integrate(): jnp.dot(mixing, rounded, preferred_element_type=jnp.float32)  7.08 us
    all_to_all x1, starting transfers between devices, local(): lax.all_to_all(moved, 'bin', split_axis=1, concat_axis=0, tiled=True)  6.68 us
    all_to_all x1, starting transfers between devices, local(): lax.all_to_all(fresh, 'bin', split_axis=0, concat_axis=1, tiled=True)  5.09 us
    unnamed x19, local copies, waits for them, and re-layouts  4.4 us
    ppermute x1, starting transfers between devices, extended(): before = lax.ppermute(last, axis, up)  4.19 us
    dot_general x1, matrix products, local(): jnp.einsum('kb,kxy->bxy', speed_table, classes, precision=lax.Precision.H...  3 us
  transfers between devices with their start and end apart: 4, of which 2 were waited for; matrix products, arithmetic and copies ran while one was open for 11% of the time, Pallas kernels for 0%

commit v1 on v0

--- a/solution.py
+++ b/solution.py
@@ -1,8 +1,12 @@
+import functools
 import math
 
 import jax
 import jax.numpy as jnp
+import numpy as np
 from jax import lax
+from jax.experimental import pallas as pl
+from jax.experimental.pallas import tpu as pltpu
 from jax.sharding import PartitionSpec as P
 
 NDIR = 32
@@ -159,6 +163,488 @@
     return (spectrum_next, forcing(stress, currents, depth_map, mask_own))
 
 
+CHUNKS = 2
+GROUP = 16
+LANES = 128
+COEF_ROWS = 160
+MESH = pl.DeviceIdType.MESH
+HIGHEST = lax.Precision.HIGHEST
+
+
+def flipped(index, k, n):
+    result, bit = 0, 1
+    while bit < n:
+        result = result + ((index // bit + k // bit) % 2) * bit
+        bit *= 2
+    return result
+
+
+def stress_matrix():
+    theta = angle_of(np.arange(NDIR, dtype=np.float64))
+    cosine, sine = np.cos(theta), np.sin(theta)
+    weights = np.stack([cosine * cosine + 1.0, cosine * sine, sine * sine + 1.0])
+    full = np.einsum("cd,fg->cfdg", weights, np.eye(NFREQ)).reshape(3 * NFREQ, NDIR * NFREQ)
+    high = full.astype(jnp.bfloat16)
+    low = (full - high.astype(np.float64)).astype(jnp.bfloat16)
+    table = np.zeros((COEF_ROWS, NDIR * NFREQ), dtype=jnp.bfloat16)
+    table[: 3 * NFREQ] = high
+    table[3 * NFREQ : 6 * NFREQ] = low
+    table[6 * NFREQ] = 1.0
+    return table
+
+
+def trig_table():
+    theta = angle_of(np.arange(NDIR, dtype=np.float64))
+    return np.abs(np.stack([np.cos(theta), np.sin(theta)])).astype(np.float32)
+
+
+def wide(tile, width):
+    return jnp.concatenate([tile] * (width // LANES), axis=1)
+
+
+def fused_kernel(
+    n,
+    spectrum_hbm,
+    mask_ref,
+    class_ref,
+    signs_ref,
+    speed_ref,
+    ratio_ref,
+    mixing_hbm,
+    growth_ref,
+    wind_ref,
+    depth_ref,
+    currents_ref,
+    trig_ref,
+    coef_hbm,
+    out_ref,
+    currents_out,
+    spectrum_v,
+    mixing_v,
+    coef_v,
+    perm,
+    energy_v,
+    flux,
+    speed_cols,
+    sign_cols,
+    growth_cols,
+    ratio_map,
+    send,
+    state,
+    total,
+    back,
+    stress,
+    halo,
+    load_sems,
+    fwd_send,
+    fwd_recv,
+    ret_send,
+    ret_recv,
+    halo_send,
+    halo_recv,
+):
+    me = lax.axis_index("bin")
+    nb, nx, ny = spectrum_v.shape
+    bins = mixing_v.shape[0]
+    width = ny // CHUNKS
+    groups = nb // GROUP
+
+    loads = [
+        pltpu.make_async_copy(src, dst, load_sems.at[i])
+        for i, (src, dst) in enumerate(
+            [(spectrum_hbm, spectrum_v), (mixing_hbm, mixing_v), (coef_hbm, coef_v)]
+        )
+    ]
+    for load in loads:
+        load.start()
+    barrier = pltpu.get_barrier_semaphore()
+
+    def greet(k, carry):
+        pl.semaphore_signal(
+            barrier, inc=1, device_id={"bin": flipped(me, k, n)}, device_id_type=MESH
+        )
+        return carry
+
+    lax.fori_loop(1, n, greet, 0)
+
+    side = GROUP * nx
+    row_id = lax.broadcasted_iota(jnp.int32, (side, side), 0)
+    col_id = lax.broadcasted_iota(jnp.int32, (side, side), 1)
+    perm[...] = jnp.where(
+        (row_id // GROUP == col_id % nx) & (row_id % GROUP == col_id // nx), 1.0, 0.0
+    ).astype(jnp.bfloat16)
+    spread = jnp.where(
+        lax.broadcasted_iota(jnp.int32, (NCLASS, NCLASS * LANES), 0)
+        == lax.broadcasted_iota(jnp.int32, (NCLASS, NCLASS * LANES), 1) // LANES,
+        1.0,
+        0.0,
+    )
+    columns = lax.dot_general(
+        speed_ref[...], spread, (((0,), (0,)), ((), ())), precision=HIGHEST,
+        preferred_element_type=jnp.float32,
+    )
+    columns = jnp.concatenate([columns] * (nb // NFREQ), axis=0)
+    for k in range(NCLASS):
+        speed_cols[k] = columns[:, k * LANES : (k + 1) * LANES]
+    pick = jnp.where(
+        lax.broadcasted_iota(jnp.int32, (nb, bins), 1)
+        == lax.broadcasted_iota(jnp.int32, (nb, bins), 0) + me * nb,
+        1.0,
+        0.0,
+    ).astype(jnp.bfloat16)
+    for axis in range(2):
+        signs = jnp.broadcast_to(
+            signs_ref[axis : axis + 1, :].astype(jnp.float32), (LANES, bins)
+        ).astype(jnp.bfloat16)
+        sign_cols[axis] = lax.dot_general(
+            pick, signs, (((1,), (1,)), ((), ())), preferred_element_type=jnp.float32
+        )
+    per_dev = nb // NFREQ
+    bin_row = lax.broadcasted_iota(jnp.int32, (nb, LANES), 0)
+    for axis in range(2):
+        column = jnp.zeros((nb, LANES), jnp.float32)
+        for d in range(per_dev):
+            column = jnp.where(bin_row // NFREQ == d, trig_ref[axis, me * per_dev + d], column)
+        sign_cols[2 + axis] = column
+
+    flux[0] = jnp.zeros((nb, ny), jnp.float32)
+    flux[nx + 1] = jnp.zeros((nb, ny), jnp.float32)
+
+    loads[0].wait()
+    for g in range(groups):
+        block = spectrum_v[g * GROUP : (g + 1) * GROUP].reshape(side, ny)
+        turned = jnp.dot(perm[...], block, preferred_element_type=jnp.float32)
+        energy_v[:, g * GROUP : (g + 1) * GROUP, :] = turned.astype(jnp.bfloat16).reshape(
+            nx, GROUP, ny
+        )
+
+    def flux_row(i, carry):
+        sea = jnp.where(mask_ref[pl.ds(i, 1), :] > 0, class_ref[pl.ds(i, 1), :], -1)
+        sea = jnp.broadcast_to(sea, (GROUP, ny))
+        for g in range(groups):
+            rows = slice(g * GROUP, (g + 1) * GROUP)
+            celerity = jnp.zeros((GROUP, ny), jnp.float32)
+            for k in range(NCLASS):
+                celerity = jnp.where(sea == k, wide(speed_cols[k, rows, :], ny), celerity)
+            flux[i + 1, rows, :] = celerity * energy_v[i, rows, :].astype(jnp.float32)
+        return carry
+
+    lax.fori_loop(0, nx, flux_row, 0)
+    pl.semaphore_wait(barrier, n - 1)
+
+    def forward(c, k):
+        return pltpu.make_async_remote_copy(
+            src_ref=send.at[c, flipped(me, k, n)],
+            dst_ref=state.at[c, 0, pl.ds(pl.multiple_of(me * nb, nb), nb), :],
+            send_sem=fwd_send.at[c, k],
+            recv_sem=fwd_recv.at[c, k],
+            device_id={"bin": flipped(me, k, n)},
+            device_id_type=MESH,
+        )
+
+    def backward(c, k):
+        return pltpu.make_async_remote_copy(
+            src_ref=state.at[c, 0, pl.ds(pl.multiple_of(flipped(me, k, n) * nb, nb), nb), :],
+            dst_ref=back.at[c, me],
+            send_sem=ret_send.at[c, k],
+            recv_sem=ret_recv.at[c, k],
+            device_id={"bin": flipped(me, k, n)},
+            device_id_type=MESH,
+        )
+
+    lane = lax.broadcasted_iota(jnp.int32, (GROUP, ny), 1)
+
+    def moved_row(t, carry):
+        k = n - 1 - t
+        j = flipped(me, k, n)
+        maskf = mask_ref[pl.ds(j, 1), :].astype(jnp.float32)
+        for g in range(groups):
+            rows = slice(g * GROUP, (g + 1) * GROUP)
+            sign_x = wide(sign_cols[0, rows, :], ny)
+            sign_y = wide(sign_cols[1, rows, :], ny)
+            cos_abs = wide(sign_cols[2, rows, :], ny)
+            sin_abs = wide(sign_cols[3, rows, :], ny)
+            here = flux[j + 1, rows, :]
+            lower_y = jnp.where(lane == 0, 0.0, pltpu.roll(here, 1, 1))
+            upper_y = jnp.where(lane == ny - 1, 0.0, pltpu.roll(here, ny - 1, 1))
+            beside_x = jnp.where(sign_x > 0, flux[j, rows, :], flux[j + 2, rows, :])
+            beside_y = jnp.where(sign_y > 0, lower_y, upper_y)
+            energy = energy_v[j, rows, :].astype(jnp.float32)
+            moved = maskf * (
+                energy - cos_abs * (here - beside_x) - sin_abs * (here - beside_y)
+            )
+            moved = moved.astype(jnp.bfloat16)
+            for c in range(CHUNKS):
+                send[c, j, rows, :] = moved[:, c * width : (c + 1) * width]
+
+        @pl.when(k > 0)
+        def _():
+            forward(0, k).start()
+
+        return carry
+
+    lax.fori_loop(0, n, moved_row, 0)
+    for c in range(1, CHUNKS):
+
+        def start_forward(t, carry):
+            forward(c, n - 1 - t).start()
+            return carry
+
+        lax.fori_loop(0, n - 1, start_forward, 0)
+    own = pl.ds(pl.multiple_of(me * nb, nb), nb)
+    for c in range(CHUNKS):
+        state[c, 0, own, :] = send[c, me]
+
+    growth_cols[...] = jnp.broadcast_to(growth_ref[...], (LANES, bins)).T
+    class_row = class_ref[pl.ds(me, 1), :]
+    one_hot = jnp.where(
+        lax.broadcasted_iota(jnp.int32, (NCLASS, ny), 0)
+        == jnp.broadcast_to(class_row, (NCLASS, ny)),
+        1.0,
+        0.0,
+    )
+    ratio_map[...] = lax.dot_general(
+        ratio_ref[...], one_hot, (((0,), (0,)), ((), ())), precision=HIGHEST,
+        preferred_element_type=jnp.float32,
+    )
+    stress[...] = jnp.zeros_like(stress)
+
+    @pl.when(me == 0)
+    def _():
+        halo[0] = jnp.zeros_like(halo[0])
+
+    @pl.when(me == n - 1)
+    def _():
+        halo[1] = jnp.zeros_like(halo[1])
+
+    loads[1].wait()
+    loads[2].wait()
+
+    tall = 256
+    for c in range(CHUNKS):
+        lanes = slice(c * width, (c + 1) * width)
+
+        def wait_forward(k, carry):
+            forward(c, k).wait_recv()
+            return carry
+
+        lax.fori_loop(1, n, wait_forward, 0)
+        wind = wind_ref[pl.ds(me, 1), lanes]
+        total[...] = state[c, 0].astype(jnp.float32)
+
+        def substep(s, carry):
+            now = s % 2
+            rounded = state[c, now]
+            for r in range(0, bins, tall):
+                mixed = jnp.dot(
+                    mixing_v[r : r + tall, :], rounded, preferred_element_type=jnp.float32
+                )
+                held = total[r : r + tall, :]
+                held = held + mixed + wide(growth_cols[r : r + tall, :], width) * wind * held
+                total[r : r + tall, :] = held
+                state[c, 1 - now, r : r + tall, :] = held.astype(jnp.bfloat16)
+            return carry
+
+        lax.fori_loop(0, SUBS, substep, 0)
+
+        def start_backward(t, carry):
+            backward(c, n - 1 - t).start()
+            return carry
+
+        lax.fori_loop(0, n - 1, start_backward, 0)
+        back[c, me] = state[c, 0, own, :]
+        weighted = jnp.dot(coef_v[...], state[c, 0], preferred_element_type=jnp.float32)
+        whole_sum = weighted[6 * NFREQ : 6 * NFREQ + 1, :]
+        for comp, offset in enumerate((0.5, 0.0, 0.5)):
+            first = comp * NFREQ
+            second = (3 + comp) * NFREQ
+            part = weighted[first : first + NFREQ, :] + weighted[second : second + NFREQ, :]
+            part = jnp.sum(ratio_map[:, lanes] * part, axis=0, keepdims=True)
+            stress[comp : comp + 1, lanes] = (part - offset * whole_sum) * STRESS_SCALE
+
+    def to_next():
+        return pltpu.make_async_remote_copy(
+            src_ref=stress,
+            dst_ref=halo.at[0],
+            send_sem=halo_send.at[0],
+            recv_sem=halo_recv.at[0],
+            device_id={"bin": (me + 1) % n},
+            device_id_type=MESH,
+        )
+
+    def to_previous():
+        return pltpu.make_async_remote_copy(
+            src_ref=stress,
+            dst_ref=halo.at[1],
+            send_sem=halo_send.at[1],
+            recv_sem=halo_recv.at[1],
+            device_id={"bin": (me + n - 1) % n},
+            device_id_type=MESH,
+        )
+
+    @pl.when(me < n - 1)
+    def _():
+        to_next().start()
+
+    @pl.when(me > 0)
+    def _():
+        to_previous().start()
+
+    def turn_back(c):
+        def wait_backward(k, carry):
+            backward(c, k).wait_recv()
+            return carry
+
+        lax.fori_loop(1, n, wait_backward, 0)
+        for g in range(groups):
+            block = back[c, :, g * GROUP : (g + 1) * GROUP, :].reshape(side, width)
+            turned = lax.dot_general(
+                perm[...], block, (((0,), (0,)), ((), ())), preferred_element_type=jnp.float32
+            )
+            out_ref[g * GROUP : (g + 1) * GROUP, :, c * width : (c + 1) * width] = turned.astype(
+                jnp.bfloat16
+            ).reshape(GROUP, nx, width)
+
+    for c in range(CHUNKS - 1):
+        turn_back(c)
+
+    @pl.when(me > 0)
+    def _():
+        to_next().wait_recv()
+
+    @pl.when(me < n - 1)
+    def _():
+        to_previous().wait_recv()
+
+    slope_x = (halo[1] - halo[0]) * 0.5
+    mine = stress[...]
+    lane8 = lax.broadcasted_iota(jnp.int32, mine.shape, 1)
+    above = jnp.where(lane8 == ny - 1, 0.0, pltpu.roll(mine, ny - 1, 1))
+    below = jnp.where(lane8 == 0, 0.0, pltpu.roll(mine, 1, 1))
+    slope_y = (above - below) * 0.5
+    depth = jnp.zeros((1, ny), jnp.float32)
+    for k in range(NCLASS):
+        depth = jnp.where(class_row == k, depth_ref[k], depth)
+    sea_row = mask_ref[pl.ds(me, 1), :].astype(jnp.float32)
+    for comp in range(2):
+        force = -(slope_x[comp : comp + 1, :] + slope_y[comp + 1 : comp + 2, :])
+        currents_out[comp] = sea_row * (currents_ref[comp] + force / depth)
+
+    turn_back(CHUNKS - 1)
+
+    def finish(k, carry):
+        for c in range(CHUNKS):
+            forward(c, k).wait_send()
+            backward(c, k).wait_send()
+        return carry
+
+    lax.fori_loop(1, n, finish, 0)
+
+    @pl.when(me < n - 1)
+    def _():
+        to_next().wait_send()
+
+    @pl.when(me > 0)
+    def _():
+        to_previous().wait_send()
+
+
+def fused(
+    n,
+    spectrum,
+    land_mask,
+    depth_class,
+    upwind_signs,
+    group_speed,
+    speed_ratio,
+    mixing,
+    growth,
+    wind_speed,
+    water_depth,
+    currents,
+):
+    nb, nx, ny = spectrum.shape
+    bins = mixing.shape[0]
+    width = ny // CHUNKS
+    vmem = pl.BlockSpec(memory_space=pltpu.VMEM)
+    smem = pl.BlockSpec(memory_space=pltpu.SMEM)
+    anywhere = pl.BlockSpec(memory_space=pl.ANY)
+    f32, bf16 = jnp.float32, jnp.bfloat16
+    dma = pltpu.SemaphoreType.DMA
+    return pl.pallas_call(
+        functools.partial(fused_kernel, n),
+        out_shape=(
+            jax.ShapeDtypeStruct(spectrum.shape, bf16),
+            jax.ShapeDtypeStruct(currents.shape, f32),
+        ),
+        in_specs=[
+            anywhere, vmem, vmem, vmem, vmem, vmem, anywhere, vmem, vmem, smem, vmem, smem, anywhere,
+        ],
+        out_specs=(vmem, vmem),
+        scratch_shapes=[
+            pltpu.VMEM((nb, nx, ny), bf16),
+            pltpu.VMEM((bins, bins), bf16),
+            pltpu.VMEM((COEF_ROWS, bins), bf16),
+            pltpu.VMEM((GROUP * nx, GROUP * nx), bf16),
+            pltpu.VMEM((nx, nb, ny), bf16),
+            pltpu.VMEM((nx + 2, nb, ny), f32),
+            pltpu.VMEM((NCLASS, nb, LANES), f32),
+            pltpu.VMEM((4, nb, LANES), f32),
+            pltpu.VMEM((bins, LANES), f32),
+            pltpu.VMEM((NFREQ, ny), f32),
+            pltpu.VMEM((CHUNKS, nx, nb, width), bf16),
+            pltpu.VMEM((CHUNKS, 2, bins, width), bf16),
+            pltpu.VMEM((bins, width), f32),
+            pltpu.VMEM((CHUNKS, nx, nb, width), bf16),
+            pltpu.VMEM((8, ny), f32),
+            pltpu.VMEM((2, 8, ny), f32),
+            dma((3,)),
+            dma((CHUNKS, n)),
+            dma((CHUNKS, n)),
+            dma((CHUNKS, n)),
+            dma((CHUNKS, n)),
+            dma((2,)),
+            dma((2,)),
+        ],
+        compiler_params=pltpu.CompilerParams(
+            collective_id=0, has_side_effects=True, vmem_limit_bytes=40 * 1024 * 1024
+        ),
+    )(
+        spectrum,
+        land_mask,
+        depth_class,
+        upwind_signs,
+        group_speed,
+        speed_ratio,
+        mixing,
+        growth.reshape(1, bins),
+        wind_speed,
+        water_depth,
+        currents,
+        jnp.asarray(trig_table()),
+        jnp.asarray(stress_matrix()),
+    )
+
+
+def fits(n, nb, nx, ny, rows):
+    return (
+        n & (n - 1) == 0
+        and rows == 1
+        and nx % GROUP == 0
+        and nb % GROUP == 0
+        and nb % NFREQ == 0
+        and ny % (CHUNKS * LANES) == 0
+    )
+
+
+def on_device(*arrays):
+    n = lax.axis_size("bin")
+    nb, nx, ny = arrays[0].shape
+    if fits(n, nb, nx, ny, arrays[-1].shape[1]):
+        return fused(n, *arrays)
+    return local(*arrays)
+
+
 def solution(mesh):
     in_specs = (
         P(("ens", "bin"), None, None),
@@ -174,4 +660,4 @@
         P("ens", "bin", None),
     )
     out_specs = (P(("ens", "bin"), None, None), P("ens", "bin", None))
-    return jax.shard_map(local, mesh=mesh, in_specs=in_specs, out_specs=out_specs, check_vma=False)
+    return jax.shard_map(on_device, mesh=mesh, in_specs=in_specs, out_specs=out_specs, check_vma=False)

time: 73.9 us -> 57.7 us (0.78)
  the two profiles are of different devices: /device:TPU:15 before, /device:TPU:0 now
where the time goes in v1:
time: 57.7 us; the launch traced here: 57.1 us
  Pallas kernels  44.6 us (77%)
  local copies, waits for them, and re-layouts  11.9 us (21%)
  between operations  0.65 us (1%)
    pallas_call x1, Pallas kernels, fused(): pl.pallas_call(functools.partial(fused_kernel, n), out_shape=(jax.ShapeDt...  44.6 us
    unnamed x26, local copies, waits for them, and re-layouts  11.2 us

profile of v1, /device:TPU:0, one launch (start us, length us, event | category | flops | bytes accessed | tf_op | source)
XLA Modules:
  0.0 57.1 jit_solution(3268384532046024018)
XLA Ops:
  0.6 0.7 %reshape.7.growth_ref = f32[1,768]{1,0:T(1,128)S(1)} reshape(f32[768]{0:T(1024)} %param.20) | data formatting | bytes 6144 | tf_op jit(solution)/shard_map/reshape | solution.py:620
  1.3 0.0 copy-start
  1.3 1.3 %copy-done = bf16[768,768]{1,0:T(8,128)(2,1)S(1)} copy-done((bf16[768,768]{1,0:T(8,128)(2,1)S(1)}, bf16[768,768]{1,0:T(8,128)(2,1)}, u32[]{:S(2)}) %copy-start) | copy-done | bytes 1179672
  2.6 0.0 copy-start.1
  2.6 1.1 %copy-done.1 = bf16[48,16,512]{2,1,0:T(8,128)(2,1)S(1)} copy-done((bf16[48,16,512]{2,1,0:T(8,128)(2,1)S(1)}, bf16[48,16,512]{2,1,0:T(8,128)(2,1)}, u32[]{:S(2)}) %copy-start.1) | copy-done | bytes 786456
  3.7 0.0 copy-start.2
  3.7 0.9 %copy-done.2 = bf16[160,768]{1,0:T(8,128)(2,1)S(1)} copy-done((bf16[160,768]{1,0:T(8,128)(2,1)S(1)}, bf16[160,768]{1,0:T(8,128)(2,1)}, u32[]{:S(2)}) %copy-start.2) | copy-done | bytes 245784
  4.7 0.0 copy-start.3
  4.7 0.8 %copy-done.3 = s32[16,512]{1,0:T(8,128)S(1)} copy-done((s32[16,512]{1,0:T(8,128)S(1)}, s32[16,512]{1,0:T(8,128)}, u32[]{:S(2)}) %copy-start.3) | copy-done | bytes 32792
  5.4 0.0 copy-start.4
  5.4 0.8 %copy-done.4 = s32[16,512]{1,0:T(8,128)S(1)} copy-done((s32[16,512]{1,0:T(8,128)S(1)}, s32[16,512]{1,0:T(8,128)}, u32[]{:S(2)}) %copy-start.4) | copy-done | bytes 32792
  6.2 0.0 copy-start.5
  6.2 0.8 %copy-done.5 = f32[16,512]{1,0:T(8,128)S(1)} copy-done((f32[16,512]{1,0:T(8,128)S(1)}, f32[16,512]{1,0:T(8,128)}, u32[]{:S(2)}) %copy-start.5) | copy-done | bytes 32792
  6.9 0.0 copy-start.6
  6.9 0.7 %copy-done.6 = s32[2,768]{1,0:T(2,128)S(1)} copy-done((s32[2,768]{1,0:T(2,128)S(1)}, s32[2,768]{1,0:T(2,128)}, u32[]{:S(2)}) %copy-start.6) | copy-done | bytes 6168
  7.6 0.0 copy-start.7
  7.6 0.7 %copy-done.7 = f32[8,24]{1,0:T(8,128)S(1)} copy-done((f32[8,24]{1,0:T(8,128)S(1)}, f32[8,24]{1,0:T(8,128)}, u32[]{:S(2)}) %copy-start.7) | copy-done | bytes 792
  8.3 0.0 copy-start.8
  8.3 0.7 %copy-done.8 = f32[8,24]{1,0:T(8,128)S(1)} copy-done((f32[8,24]{1,0:T(8,128)S(1)}, f32[8,24]{1,0:T(8,128)}, u32[]{:S(2)}) %copy-start.8) | copy-done | bytes 792
  9.0 0.0 copy-start.9
  9.0 0.7 %copy-done.9 = f32[2,1,512]{2,1,0:T(1,128)S(1)} copy-done((f32[2,1,512]{2,1,0:T(1,128)S(1)}, f32[2,1,512]{2,1,0:T(1,128)}, u32[]{:S(2)}) %copy-start.9) | copy-done | bytes 4120
  9.7 0.0 copy-start.10
  9.7 0.7 %copy-done.10 = f32[2,32]{1,0:T(2,128)S(1)} copy-done((f32[2,32]{1,0:T(2,128)S(1)}, f32[2,32]{1,0:T(2,128)}, u32[]{:S(2)}) %copy-start.10) | copy-done | bytes 280
  10.4 0.0 copy-start.11
  10.4 0.7 %copy-done.11 = f32[8]{0:T(128)S(1)} copy-done((f32[8]{0:T(128)S(1)}, f32[8]{0:T(128)}, u32[]{:S(2)}) %copy-start.11) | copy-done | bytes 56
  11.0 44.6 %shard_map.140 = (bf16[48,16,512]{2,1,0:T(8,128)(2,1)S(1)}, f32[2,1,512]{2,1,0:T(1,128)S(1)}) custom-call(bf16[48,16,512]{2,1,0:T(8,128)(2,1)S(1)} %copy-done.1, s32[16,512]{1,0:T(8,128)S(1)} %copy-done.3, s32[16,512]{1,0:T(8,128)S(1)} %copy-done.4, s32[2,768]{1,0:T(2,128)S(1)} %copy-done.6, f32[8,24]{1,0:T(8,128)S(1)} %copy-done.7, f32[8,24]{1,0:T(8,128)S(1)} %copy-done.8, ...), custom_call_target="tpu_custom_call" | custom-call | tf_op jit(solution)/shard_map/pallas_call | solution.py:574
  55.6 0.9 %copy.17 = bf16[48,16,512]{2,1,0:T(8,128)(2,1)} copy(bf16[48,16,512]{2,1,0:T(8,128)(2,1)S(1)} %get-tuple-element.4) | data formatting | bytes 1572864
  56.5 0.6 %copy.18 = f32[2,1,512]{2,1,0:T(1,128)} copy(f32[2,1,512]{2,1,0:T(1,128)S(1)} %get-tuple-element.5) | data formatting | bytes 8192
Async XLA Ops:
  1.3 1.3 %copy-start = (bf16[768,768]{1,0:T(8,128)(2,1)S(1)}, bf16[768,768]{1,0:T(8,128)(2,1)}, u32[]{:S(2)}) copy-start(bf16[768,768]{1,0:T(8,128)(2,1)} %mixing_hbm.1) | copy-start | bytes 3538948
  2.6 1.1 %copy-start.1 = (bf16[48,16,512]{2,1,0:T(8,128)(2,1)S(1)}, bf16[48,16,512]{2,1,0:T(8,128)(2,1)}, u32[]{:S(2)}) copy-start(bf16[48,16,512]{2,1,0:T(8,128)(2,1)} %spectrum_hbm.1) | copy-start | bytes 2359300
  3.7 0.9 %copy-start.2 = (bf16[160,768]{1,0:T(8,128)(2,1)S(1)}, bf16[160,768]{1,0:T(8,128)(2,1)}, u32[]{:S(2)}) copy-start(bf16[160,768]{1,0:T(8,128)(2,1)} %constant.5.clone.coef_hbm) | copy-start | bytes 737284
  4.7 0.8 %copy-start.3 = (s32[16,512]{1,0:T(8,128)S(1)}, s32[16,512]{1,0:T(8,128)}, u32[]{:S(2)}) copy-start(s32[16,512]{1,0:T(8,128)} %mask_ref.1) | copy-start | bytes 98308
  5.4 0.8 %copy-start.4 = (s32[16,512]{1,0:T(8,128)S(1)}, s32[16,512]{1,0:T(8,128)}, u32[]{:S(2)}) copy-start(s32[16,512]{1,0:T(8,128)} %class_ref.1) | copy-start | bytes 98308
  6.2 0.8 %copy-start.5 = (f32[16,512]{1,0:T(8,128)S(1)}, f32[16,512]{1,0:T(8,128)}, u32[]{:S(2)}) copy-start(f32[16,512]{1,0:T(8,128)} %wind_ref.1) | copy-start | bytes 98308
  6.9 0.7 %copy-start.6 = (s32[2,768]{1,0:T(2,128)S(1)}, s32[2,768]{1,0:T(2,128)}, u32[]{:S(2)}) copy-start(s32[2,768]{1,0:T(2,128)} %signs_ref.1) | copy-start | bytes 18436
  7.6 0.7 %copy-start.7 = (f32[8,24]{1,0:T(8,128)S(1)}, f32[8,24]{1,0:T(8,128)}, u32[]{:S(2)}) copy-start(f32[8,24]{1,0:T(8,128)} %speed_ref.1) | copy-start | bytes 2308
  8.3 0.7 %copy-start.8 = (f32[8,24]{1,0:T(8,128)S(1)}, f32[8,24]{1,0:T(8,128)}, u32[]{:S(2)}) copy-start(f32[8,24]{1,0:T(8,128)} %ratio_ref.1) | copy-start | bytes 2308
  9.0 0.7 %copy-start.9 = (f32[2,1,512]{2,1,0:T(1,128)S(1)}, f32[2,1,512]{2,1,0:T(1,128)}, u32[]{:S(2)}) copy-start(f32[2,1,512]{2,1,0:T(1,128)} %currents_ref.1) | copy-start | bytes 12292
  9.7 0.7 %copy-start.10 = (f32[2,32]{1,0:T(2,128)S(1)}, f32[2,32]{1,0:T(2,128)}, u32[]{:S(2)}) copy-start(f32[2,32]{1,0:T(2,128)} %constant.4.clone.trig_ref) | copy-start | bytes 772
  10.4 0.7 %copy-start.11 = (f32[8]{0:T(128)S(1)}, f32[8]{0:T(128)}, u32[]{:S(2)}) copy-start(f32[8]{0:T(128)} %depth_ref.1) | copy-start | bytes 100

commit v2 on v1

--- a/solution.py
+++ b/solution.py
@@ -183,13 +183,11 @@
     theta = angle_of(np.arange(NDIR, dtype=np.float64))
     cosine, sine = np.cos(theta), np.sin(theta)
     weights = np.stack([cosine * cosine + 1.0, cosine * sine, sine * sine + 1.0])
-    full = np.einsum("cd,fg->cfdg", weights, np.eye(NFREQ)).reshape(3 * NFREQ, NDIR * NFREQ)
-    high = full.astype(jnp.bfloat16)
-    low = (full - high.astype(np.float64)).astype(jnp.bfloat16)
-    table = np.zeros((COEF_ROWS, NDIR * NFREQ), dtype=jnp.bfloat16)
-    table[: 3 * NFREQ] = high
-    table[3 * NFREQ : 6 * NFREQ] = low
-    table[6 * NFREQ] = 1.0
+    full = np.repeat(weights, NFREQ, axis=1)
+    high = full.astype(jnp.bfloat16).astype(np.float64)
+    table = np.ones((8, NDIR * NFREQ), dtype=np.float32)
+    table[:3] = high
+    table[3:6] = (full - high).astype(jnp.bfloat16)
     return table
 
 
@@ -205,22 +203,35 @@
 def fused_kernel(
     n,
     spectrum_hbm,
+    mask_hbm,
+    class_hbm,
+    signs_hbm,
+    speed_hbm,
+    ratio_hbm,
+    mixing_hbm,
+    growth_hbm,
+    wind_hbm,
+    depth_hbm,
+    currents_hbm,
+    trig_hbm,
+    weight_hbm,
+    out_hbm,
+    currents_out_hbm,
+    out_ref,
+    currents_out,
+    spectrum_v,
     mask_ref,
     class_ref,
     signs_ref,
     speed_ref,
     ratio_ref,
-    mixing_hbm,
+    mixing_v,
     growth_ref,
     wind_ref,
     depth_ref,
     currents_ref,
     trig_ref,
-    coef_hbm,
-    out_ref,
-    currents_out,
-    spectrum_v,
-    mixing_v,
+    weight_ref,
     coef_v,
     perm,
     energy_v,
@@ -236,6 +247,7 @@
     stress,
     halo,
     load_sems,
+    store_sems,
     fwd_send,
     fwd_recv,
     ret_send,
@@ -252,7 +264,21 @@
     loads = [
         pltpu.make_async_copy(src, dst, load_sems.at[i])
         for i, (src, dst) in enumerate(
-            [(spectrum_hbm, spectrum_v), (mixing_hbm, mixing_v), (coef_hbm, coef_v)]
+            [
+                (spectrum_hbm, spectrum_v),
+                (speed_hbm, speed_ref),
+                (signs_hbm, signs_ref),
+                (trig_hbm, trig_ref),
+                (mask_hbm, mask_ref),
+                (class_hbm, class_ref),
+                (growth_hbm, growth_ref.at[0]),
+                (ratio_hbm, ratio_ref),
+                (wind_hbm, wind_ref),
+                (mixing_hbm, mixing_v),
+                (weight_hbm, weight_ref),
+                (depth_hbm, depth_ref),
+                (currents_hbm, currents_ref),
+            ]
         )
     ]
     for load in loads:
@@ -267,6 +293,8 @@
 
     lax.fori_loop(1, n, greet, 0)
 
+    for load in loads[1:4]:
+        load.wait()
     side = GROUP * nx
     row_id = lax.broadcasted_iota(jnp.int32, (side, side), 0)
     col_id = lax.broadcasted_iota(jnp.int32, (side, side), 1)
@@ -317,6 +345,9 @@
         energy_v[:, g * GROUP : (g + 1) * GROUP, :] = turned.astype(jnp.bfloat16).reshape(
             nx, GROUP, ny
         )
+
+    loads[4].wait()
+    loads[5].wait()
 
     def flux_row(i, carry):
         sea = jnp.where(mask_ref[pl.ds(i, 1), :] > 0, class_ref[pl.ds(i, 1), :], -1)
@@ -395,6 +426,8 @@
     for c in range(CHUNKS):
         state[c, 0, own, :] = send[c, me]
 
+    for load in loads[6:]:
+        load.wait()
     growth_cols[...] = jnp.broadcast_to(growth_ref[...], (LANES, bins)).T
     class_row = class_ref[pl.ds(me, 1), :]
     one_hot = jnp.where(
@@ -408,6 +441,13 @@
         preferred_element_type=jnp.float32,
     )
     stress[...] = jnp.zeros_like(stress)
+    same_freq = (
+        lax.broadcasted_iota(jnp.int32, (NFREQ, bins), 1) % NFREQ
+        == lax.broadcasted_iota(jnp.int32, (NFREQ, bins), 0)
+    )
+    weights = [jnp.where(same_freq, weight_ref[i : i + 1, :], 0.0) for i in range(6)]
+    ones = jnp.broadcast_to(weight_ref[6:7, :], (COEF_ROWS - 6 * NFREQ, bins))
+    coef_v[...] = jnp.concatenate(weights + [ones], axis=0).astype(jnp.bfloat16)
 
     @pl.when(me == 0)
     def _():
@@ -416,9 +456,6 @@
     @pl.when(me == n - 1)
     def _():
         halo[1] = jnp.zeros_like(halo[1])
-
-    loads[1].wait()
-    loads[2].wait()
 
     tall = 256
     for c in range(CHUNKS):
@@ -490,6 +527,12 @@
     def _():
         to_previous().start()
 
+    def store(c):
+        lanes = pl.ds(c * width, width)
+        return pltpu.make_async_copy(
+            out_ref.at[:, :, lanes], out_hbm.at[:, :, lanes], store_sems.at[c]
+        )
+
     def turn_back(c):
         def wait_backward(k, carry):
             backward(c, k).wait_recv()
@@ -504,6 +547,7 @@
             out_ref[g * GROUP : (g + 1) * GROUP, :, c * width : (c + 1) * width] = turned.astype(
                 jnp.bfloat16
             ).reshape(GROUP, nx, width)
+        store(c).start()
 
     for c in range(CHUNKS - 1):
         turn_back(c)
@@ -530,6 +574,10 @@
         force = -(slope_x[comp : comp + 1, :] + slope_y[comp + 1 : comp + 2, :])
         currents_out[comp] = sea_row * (currents_ref[comp] + force / depth)
 
+    store_currents = pltpu.make_async_copy(
+        currents_out, currents_out_hbm, store_sems.at[CHUNKS]
+    )
+    store_currents.start()
     turn_back(CHUNKS - 1)
 
     def finish(k, carry):
@@ -547,6 +595,10 @@
     @pl.when(me > 0)
     def _():
         to_previous().wait_send()
+
+    store_currents.wait()
+    for c in range(CHUNKS):
+        store(c).wait()
 
 
 def fused(
@@ -566,9 +618,7 @@
     nb, nx, ny = spectrum.shape
     bins = mixing.shape[0]
     width = ny // CHUNKS
-    vmem = pl.BlockSpec(memory_space=pltpu.VMEM)
-    smem = pl.BlockSpec(memory_space=pltpu.SMEM)
-    anywhere = pl.BlockSpec(memory_space=pl.ANY)
+    hbm = pl.BlockSpec(memory_space=pltpu.HBM)
     f32, bf16 = jnp.float32, jnp.bfloat16
     dma = pltpu.SemaphoreType.DMA
     return pl.pallas_call(
@@ -577,13 +627,24 @@
             jax.ShapeDtypeStruct(spectrum.shape, bf16),
             jax.ShapeDtypeStruct(currents.shape, f32),
         ),
-        in_specs=[
-            anywhere, vmem, vmem, vmem, vmem, vmem, anywhere, vmem, vmem, smem, vmem, smem, anywhere,
-        ],
-        out_specs=(vmem, vmem),
+        in_specs=[hbm] * 13,
+        out_specs=(hbm, hbm),
         scratch_shapes=[
             pltpu.VMEM((nb, nx, ny), bf16),
+            pltpu.VMEM(currents.shape, f32),
+            pltpu.VMEM((nb, nx, ny), bf16),
+            pltpu.VMEM(land_mask.shape, jnp.int32),
+            pltpu.VMEM(depth_class.shape, jnp.int32),
+            pltpu.VMEM(upwind_signs.shape, jnp.int32),
+            pltpu.VMEM(group_speed.shape, f32),
+            pltpu.VMEM(speed_ratio.shape, f32),
             pltpu.VMEM((bins, bins), bf16),
+            pltpu.VMEM((1, bins), f32),
+            pltpu.VMEM(wind_speed.shape, f32),
+            pltpu.SMEM(water_depth.shape, f32),
+            pltpu.VMEM(currents.shape, f32),
+            pltpu.SMEM((2, NDIR), f32),
+            pltpu.VMEM((8, bins), f32),
             pltpu.VMEM((COEF_ROWS, bins), bf16),
             pltpu.VMEM((GROUP * nx, GROUP * nx), bf16),
             pltpu.VMEM((nx, nb, ny), bf16),
@@ -598,7 +659,8 @@
             pltpu.VMEM((CHUNKS, nx, nb, width), bf16),
             pltpu.VMEM((8, ny), f32),
             pltpu.VMEM((2, 8, ny), f32),
-            dma((3,)),
+            dma((13,)),
+            dma((CHUNKS + 1,)),
             dma((CHUNKS, n)),
             dma((CHUNKS, n)),
             dma((CHUNKS, n)),
@@ -607,7 +669,7 @@
             dma((2,)),
         ],
         compiler_params=pltpu.CompilerParams(
-            collective_id=0, has_side_effects=True, vmem_limit_bytes=40 * 1024 * 1024
+            collective_id=0, has_side_effects=True, vmem_limit_bytes=64 * 1024 * 1024
         ),
     )(
         spectrum,
@@ -617,13 +679,37 @@
         group_speed,
         speed_ratio,
         mixing,
-        growth.reshape(1, bins),
+        growth,
         wind_speed,
         water_depth,
         currents,
         jnp.asarray(trig_table()),
         jnp.asarray(stress_matrix()),
     )
+
+
+def hand_on_kernel(*refs):
+    sems = refs[-1]
+    count = (len(refs) - 1) // 2
+    copies = [
+        pltpu.make_async_copy(refs[i], refs[count + i], sems.at[i]) for i in range(count)
+    ]
+    for copy in copies:
+        copy.start()
+    for copy in copies:
+        copy.wait()
+
+
+def hand_on(*arrays):
+    hbm = pl.BlockSpec(memory_space=pltpu.HBM)
+    return pl.pallas_call(
+        hand_on_kernel,
+        out_shape=tuple(jax.ShapeDtypeStruct(a.shape, a.dtype) for a in arrays),
+        in_specs=[hbm] * len(arrays),
+        out_specs=tuple([hbm] * len(arrays)),
+        scratch_shapes=[pltpu.SemaphoreType.DMA((len(arrays),))],
+        compiler_params=pltpu.CompilerParams(vmem_limit_bytes=64 * 1024 * 1024),
+    )(*arrays)
 
 
 def fits(n, nb, nx, ny, rows):
@@ -641,7 +727,7 @@
     n = lax.axis_size("bin")
     nb, nx, ny = arrays[0].shape
     if fits(n, nb, nx, ny, arrays[-1].shape[1]):
-        return fused(n, *arrays)
+        return hand_on(*fused(n, *arrays))
     return local(*arrays)
 
 

time: 57.7 us -> 70 us (1.21)
  Pallas kernels: 44.6 us -> 69.3 us
  local copies, waits for them, and re-layouts: 11.9 us -> 0 us
    pallas_call x0 -> x1, Pallas kernels: none -> 25.1 us  [hand_on(): pl.pallas_call(hand_on_kernel, out_shape=tuple((jax.ShapeDtypeStruct(a.sh...]
    unnamed x26 -> x0, local copies, waits for them, and re-layouts: 11.2 us -> none
where the time goes in v2:
time: 70 us; the launch traced here: 69.9 us
  Pallas kernels  69.3 us (99%)
    pallas_call x1, Pallas kernels, fused(): pl.pallas_call(functools.partial(fused_kernel, n), out_shape=(jax.ShapeDt...  44.2 us
    pallas_call x1, Pallas kernels, hand_on(): pl.pallas_call(hand_on_kernel, out_shape=tuple((jax.ShapeDtypeStruct(a.sh...  25.1 us

profile of v2, /device:TPU:0, one launch (start us, length us, event | category | flops | bytes accessed | tf_op | source)
XLA Modules:
  0.0 69.9 jit_solution(2828506567010879046)
XLA Ops:
  0.6 44.2 %shard_map.140 = (bf16[48,16,512]{2,1,0:T(8,128)(2,1)}, f32[2,1,512]{2,1,0:T(1,128)}) custom-call(bf16[48,16,512]{2,1,0:T(8,128)(2,1)} %spectrum_hbm.1, s32[16,512]{1,0:T(8,128)} %mask_hbm.1, s32[16,512]{1,0:T(8,128)} %class_hbm.1, s32[2,768]{1,0:T(2,128)} %signs_hbm.1, f32[8,24]{1,0:T(8,128)} %speed_hbm.1, f32[8,24]{1,0:T(8,128)} %ratio_hbm.1, ...), custom_call_target="tpu_custom_call" | custom-call | tf_op jit(solution)/shard_map/pallas_call | solution.py:624
  44.8 25.1 %shard_map.141 = (bf16[48,16,512]{2,1,0:T(8,128)(2,1)}, f32[2,1,512]{2,1,0:T(1,128)}) custom-call(bf16[48,16,512]{2,1,0:T(8,128)(2,1)} %get-tuple-element.4.refs_0_, f32[2,1,512]{2,1,0:T(1,128)} %get-tuple-element.5.refs_1_), custom_call_target="tpu_custom_call" | custom-call | tf_op jit(solution)/shard_map/pallas_call | solution.py:705

commit v3 on v2

--- a/solution.py
+++ b/solution.py
@@ -196,6 +196,14 @@
     return np.abs(np.stack([np.cos(theta), np.sin(theta)])).astype(np.float32)
 
 
+def turning(outer, inner):
+    side = outer * inner
+    row_id = lax.broadcasted_iota(jnp.int32, (side, side), 0)
+    col_id = lax.broadcasted_iota(jnp.int32, (side, side), 1)
+    hit = (row_id // inner == col_id % outer) & (row_id % inner == col_id // outer)
+    return jnp.where(hit, 1.0, 0.0).astype(jnp.bfloat16)
+
+
 def wide(tile, width):
     return jnp.concatenate([tile] * (width // LANES), axis=1)
 
@@ -215,9 +223,8 @@
     currents_hbm,
     trig_hbm,
     weight_hbm,
-    out_hbm,
+    back,
     currents_out_hbm,
-    out_ref,
     currents_out,
     spectrum_v,
     mask_ref,
@@ -243,7 +250,6 @@
     send,
     state,
     total,
-    back,
     stress,
     halo,
     load_sems,
@@ -296,11 +302,7 @@
     for load in loads[1:4]:
         load.wait()
     side = GROUP * nx
-    row_id = lax.broadcasted_iota(jnp.int32, (side, side), 0)
-    col_id = lax.broadcasted_iota(jnp.int32, (side, side), 1)
-    perm[...] = jnp.where(
-        (row_id // GROUP == col_id % nx) & (row_id % GROUP == col_id // nx), 1.0, 0.0
-    ).astype(jnp.bfloat16)
+    perm[...] = turning(nx, GROUP)
     spread = jnp.where(
         lax.broadcasted_iota(jnp.int32, (NCLASS, NCLASS * LANES), 0)
         == lax.broadcasted_iota(jnp.int32, (NCLASS, NCLASS * LANES), 1) // LANES,
@@ -381,6 +383,13 @@
             recv_sem=ret_recv.at[c, k],
             device_id={"bin": flipped(me, k, n)},
             device_id_type=MESH,
+        )
+
+    def keep(c):
+        return pltpu.make_async_copy(
+            state.at[c, 0, pl.ds(pl.multiple_of(me * nb, nb), nb), :],
+            back.at[c, me],
+            store_sems.at[c],
         )
 
     lane = lax.broadcasted_iota(jnp.int32, (GROUP, ny), 1)
@@ -489,7 +498,7 @@
             return carry
 
         lax.fori_loop(0, n - 1, start_backward, 0)
-        back[c, me] = state[c, 0, own, :]
+        keep(c).start()
         weighted = jnp.dot(coef_v[...], state[c, 0], preferred_element_type=jnp.float32)
         whole_sum = weighted[6 * NFREQ : 6 * NFREQ + 1, :]
         for comp, offset in enumerate((0.5, 0.0, 0.5)):
@@ -526,31 +535,6 @@
     @pl.when(me > 0)
     def _():
         to_previous().start()
-
-    def store(c):
-        lanes = pl.ds(c * width, width)
-        return pltpu.make_async_copy(
-            out_ref.at[:, :, lanes], out_hbm.at[:, :, lanes], store_sems.at[c]
-        )
-
-    def turn_back(c):
-        def wait_backward(k, carry):
-            backward(c, k).wait_recv()
-            return carry
-
-        lax.fori_loop(1, n, wait_backward, 0)
-        for g in range(groups):
-            block = back[c, :, g * GROUP : (g + 1) * GROUP, :].reshape(side, width)
-            turned = lax.dot_general(
-                perm[...], block, (((0,), (0,)), ((), ())), preferred_element_type=jnp.float32
-            )
-            out_ref[g * GROUP : (g + 1) * GROUP, :, c * width : (c + 1) * width] = turned.astype(
-                jnp.bfloat16
-            ).reshape(GROUP, nx, width)
-        store(c).start()
-
-    for c in range(CHUNKS - 1):
-        turn_back(c)
 
     @pl.when(me > 0)
     def _():
@@ -578,7 +562,13 @@
         currents_out, currents_out_hbm, store_sems.at[CHUNKS]
     )
     store_currents.start()
-    turn_back(CHUNKS - 1)
+
+    def wait_backward(k, carry):
+        for c in range(CHUNKS):
+            backward(c, k).wait_recv()
+        return carry
+
+    lax.fori_loop(1, n, wait_backward, 0)
 
     def finish(k, carry):
         for c in range(CHUNKS):
@@ -598,7 +588,7 @@
 
     store_currents.wait()
     for c in range(CHUNKS):
-        store(c).wait()
+        keep(c).wait()
 
 
 def fused(
@@ -624,13 +614,12 @@
     return pl.pallas_call(
         functools.partial(fused_kernel, n),
         out_shape=(
-            jax.ShapeDtypeStruct(spectrum.shape, bf16),
+            jax.ShapeDtypeStruct((CHUNKS, nx, nb, width), bf16),
             jax.ShapeDtypeStruct(currents.shape, f32),
         ),
         in_specs=[hbm] * 13,
         out_specs=(hbm, hbm),
         scratch_shapes=[
-            pltpu.VMEM((nb, nx, ny), bf16),
             pltpu.VMEM(currents.shape, f32),
             pltpu.VMEM((nb, nx, ny), bf16),
             pltpu.VMEM(land_mask.shape, jnp.int32),
@@ -656,7 +645,6 @@
             pltpu.VMEM((CHUNKS, nx, nb, width), bf16),
             pltpu.VMEM((CHUNKS, 2, bins, width), bf16),
             pltpu.VMEM((bins, width), f32),
-            pltpu.VMEM((CHUNKS, nx, nb, width), bf16),
             pltpu.VMEM((8, ny), f32),
             pltpu.VMEM((2, 8, ny), f32),
             dma((13,)),
@@ -688,28 +676,54 @@
     )
 
 
-def hand_on_kernel(*refs):
-    sems = refs[-1]
-    count = (len(refs) - 1) // 2
-    copies = [
-        pltpu.make_async_copy(refs[i], refs[count + i], sems.at[i]) for i in range(count)
+def turn_kernel(back, currents_in, fresh_out, currents_out, back_v, fresh_v, currents_v, sems):
+    chunks, nx, nb, width = back_v.shape
+    groups = [pl.ds(g, GROUP) for g in range(0, nb, GROUP)]
+    loads = [pltpu.make_async_copy(back.at[c], back_v.at[c], sems.at[0, c]) for c in range(chunks)]
+    stores = [
+        pltpu.make_async_copy(fresh_v.at[g], fresh_out.at[g], sems.at[1, i])
+        for i, g in enumerate(groups)
     ]
-    for copy in copies:
-        copy.start()
-    for copy in copies:
-        copy.wait()
-
-
-def hand_on(*arrays):
+    load_currents = pltpu.make_async_copy(currents_in, currents_v, sems.at[0, chunks])
+    store_currents = pltpu.make_async_copy(currents_v, currents_out, sems.at[1, len(groups)])
+    for load in loads:
+        load.start()
+    load_currents.start()
+    perm = turning(GROUP, nx)
+    load_currents.wait()
+    store_currents.start()
+    for load in loads:
+        load.wait()
+    for g, store in zip(groups, stores):
+        for c in range(chunks):
+            block = back_v[c, :, g, :].reshape(nx * GROUP, width)
+            turned = jnp.dot(perm, block, preferred_element_type=jnp.float32)
+            fresh_v[g, :, c * width : (c + 1) * width] = turned.astype(jnp.bfloat16).reshape(
+                GROUP, nx, width
+            )
+        store.start()
+    for store in stores + [store_currents]:
+        store.wait()
+
+
+def turn(back, currents):
+    chunks, nx, nb, width = back.shape
     hbm = pl.BlockSpec(memory_space=pltpu.HBM)
+    fresh = jax.ShapeDtypeStruct((nb, nx, chunks * width), back.dtype)
+    count = max(chunks, nb // GROUP) + 1
     return pl.pallas_call(
-        hand_on_kernel,
-        out_shape=tuple(jax.ShapeDtypeStruct(a.shape, a.dtype) for a in arrays),
-        in_specs=[hbm] * len(arrays),
-        out_specs=tuple([hbm] * len(arrays)),
-        scratch_shapes=[pltpu.SemaphoreType.DMA((len(arrays),))],
+        turn_kernel,
+        out_shape=(fresh, jax.ShapeDtypeStruct(currents.shape, currents.dtype)),
+        in_specs=[hbm, hbm],
+        out_specs=(hbm, hbm),
+        scratch_shapes=[
+            pltpu.VMEM(back.shape, back.dtype),
+            pltpu.VMEM(fresh.shape, fresh.dtype),
+            pltpu.VMEM(currents.shape, currents.dtype),
+            pltpu.SemaphoreType.DMA((2, count)),
+        ],
         compiler_params=pltpu.CompilerParams(vmem_limit_bytes=64 * 1024 * 1024),
-    )(*arrays)
+    )(back, currents)
 
 
 def fits(n, nb, nx, ny, rows):
@@ -727,7 +741,7 @@
     n = lax.axis_size("bin")
     nb, nx, ny = arrays[0].shape
     if fits(n, nb, nx, ny, arrays[-1].shape[1]):
-        return hand_on(*fused(n, *arrays))
+        return turn(*fused(n, *arrays))
     return local(*arrays)
 
 

time: 70 us -> 46.5 us (0.66)
  Pallas kernels: 69.3 us -> 45.7 us
    pallas_call x1, Pallas kernels: 25.1 us -> 2.3 us  [turn(): pl.pallas_call(turn_kernel, out_shape=(fresh, jax.ShapeDtypeStruct(curren...]
    pallas_call x1, Pallas kernels: 44.2 us -> 43.4 us  [fused(): pl.pallas_call(functools.partial(fused_kernel, n), out_shape=(jax.ShapeDt...]
where the time goes in v3:
time: 46.5 us; the launch traced here: 46.3 us
  Pallas kernels  45.7 us (98%)
  between operations  0.64 us (1%)
    pallas_call x1, Pallas kernels, fused(): pl.pallas_call(functools.partial(fused_kernel, n), out_shape=(jax.ShapeDt...  43.4 us
    pallas_call x1, Pallas kernels, turn(): pl.pallas_call(turn_kernel, out_shape=(fresh, jax.ShapeDtypeStruct(curren...  2.3 us

profile of v3, /device:TPU:0, one launch (start us, length us, event | category | flops | bytes accessed | tf_op | source)
XLA Modules:
  0.0 46.3 jit_solution(12782097569588928567)
XLA Ops:
  0.6 43.4 %shard_map.140 = (bf16[2,16,48,256]{3,2,1,0:T(8,128)(2,1)}, f32[2,1,512]{2,1,0:T(1,128)}) custom-call(bf16[48,16,512]{2,1,0:T(8,128)(2,1)} %spectrum_hbm.1, s32[16,512]{1,0:T(8,128)} %mask_hbm.1, s32[16,512]{1,0:T(8,128)} %class_hbm.1, s32[2,768]{1,0:T(2,128)} %signs_hbm.1, f32[8,24]{1,0:T(8,128)} %speed_hbm.1, f32[8,24]{1,0:T(8,128)} %ratio_hbm.1, ...), custom_call_target="tpu_custom_call" | custom-call | tf_op jit(solution)/shard_map/pallas_call | solution.py:614
  44.0 2.3 %shard_map.141 = (bf16[48,16,512]{2,1,0:T(8,128)(2,1)}, f32[2,1,512]{2,1,0:T(1,128)}) custom-call(bf16[2,16,48,256]{3,2,1,0:T(8,128)(2,1)} %get-tuple-element.4.back, f32[2,1,512]{2,1,0:T(1,128)} %get-tuple-element.5.currents_in), custom_call_target="tpu_custom_call" | custom-call | tf_op jit(solution)/shard_map/pallas_call | solution.py:714

commit v4 on v3

--- a/solution.py
+++ b/solution.py
@@ -164,6 +164,7 @@
 
 
 CHUNKS = 2
+PLANES = 4
 GROUP = 16
 LANES = 128
 COEF_ROWS = 160
@@ -260,6 +261,7 @@
     ret_recv,
     halo_send,
     halo_recv,
+    relay,
 ):
     me = lax.axis_index("bin")
     nb, nx, ny = spectrum_v.shape
@@ -291,13 +293,37 @@
         load.start()
     barrier = pltpu.get_barrier_semaphore()
 
-    def greet(k, carry):
-        pl.semaphore_signal(
-            barrier, inc=1, device_id={"bin": flipped(me, k, n)}, device_id_type=MESH
-        )
+    span = n // PLANES
+    plane = me // span
+    inner = (plane > 0) & (plane < PLANES - 1)
+    outer = (plane == 0) | (plane == PLANES - 1)
+    outward = jnp.where(plane == 1, me - span, me + span)
+    inward = jnp.where(plane == 1, me + span, me - span)
+
+    def tell(semaphore, device):
+        pl.semaphore_signal(semaphore, inc=1, device_id={"bin": device}, device_id_type=MESH)
+
+    def greet_lower(q, carry):
+        tell(barrier, (plane - 1) * span + q)
         return carry
 
-    lax.fori_loop(1, n, greet, 0)
+    def greet_upper(q, carry):
+        tell(barrier, (plane + 1) * span + q)
+        return carry
+
+    def greet_own(k, carry):
+        tell(barrier, flipped(me, k, n))
+        return carry
+
+    @pl.when(plane > 0)
+    def _():
+        lax.fori_loop(0, span, greet_lower, 0)
+
+    @pl.when(plane < PLANES - 1)
+    def _():
+        lax.fori_loop(0, span, greet_upper, 0)
+
+    lax.fori_loop(1, span, greet_own, 0)
 
     for load in loads[1:4]:
         load.wait()
@@ -363,7 +389,22 @@
         return carry
 
     lax.fori_loop(0, nx, flux_row, 0)
-    pl.semaphore_wait(barrier, n - 1)
+
+    @pl.when(outer)
+    def _():
+        pl.semaphore_wait(barrier, 2 * span - 1)
+
+    @pl.when(inner)
+    def _():
+        pl.semaphore_wait(barrier, 3 * span - 1)
+        tell(relay.at[0], inward)
+        tell(relay.at[0], outward)
+
+    def far_first(t):
+        stage = t // span
+        block = PLANES - 1 - stage
+        block = jnp.where(inner & (stage < 2), PLANES - 2 + stage, block)
+        return block * span + span - 1 - t % span
 
     def forward(c, k):
         return pltpu.make_async_remote_copy(
@@ -395,7 +436,13 @@
     lane = lax.broadcasted_iota(jnp.int32, (GROUP, ny), 1)
 
     def moved_row(t, carry):
-        k = n - 1 - t
+        stage = t // span
+        block = jnp.where(
+            inner,
+            PLANES - 1 - stage,
+            jnp.where(stage == PLANES - 1, 0, stage + 1),
+        )
+        k = block * span + span - 1 - t % span
         j = flipped(me, k, n)
         maskf = mask_ref[pl.ds(j, 1), :].astype(jnp.float32)
         for g in range(groups):
@@ -417,6 +464,18 @@
             for c in range(CHUNKS):
                 send[c, j, rows, :] = moved[:, c * width : (c + 1) * width]
 
+        @pl.when(t == span)
+        def _():
+            pl.semaphore_wait(relay.at[0], 1)
+
+            @pl.when(inner)
+            def _():
+                tell(relay.at[1], outward)
+
+        @pl.when((t == 2 * span) & outer)
+        def _():
+            pl.semaphore_wait(relay.at[1], 1)
+
         @pl.when(k > 0)
         def _():
             forward(0, k).start()
@@ -494,7 +553,7 @@
         lax.fori_loop(0, SUBS, substep, 0)
 
         def start_backward(t, carry):
-            backward(c, n - 1 - t).start()
+            backward(c, far_first(t)).start()
             return carry
 
         lax.fori_loop(0, n - 1, start_backward, 0)
@@ -655,6 +714,7 @@
             dma((CHUNKS, n)),
             dma((2,)),
             dma((2,)),
+            pltpu.SemaphoreType.REGULAR((2,)),
         ],
         compiler_params=pltpu.CompilerParams(
             collective_id=0, has_side_effects=True, vmem_limit_bytes=64 * 1024 * 1024
@@ -729,6 +789,7 @@
 def fits(n, nb, nx, ny, rows):
     return (
         n & (n - 1) == 0
+        and n >= 2 * PLANES
         and rows == 1
         and nx % GROUP == 0
         and nb % GROUP == 0

time: 46.5 us -> 44.7 us (0.961)
  Pallas kernels: 45.7 us -> 43.9 us
    pallas_call x1, Pallas kernels: 43.4 us -> 41.6 us  [fused(): pl.pallas_call(functools.partial(fused_kernel, n), out_shape=(jax.ShapeDt...]
where the time goes in v4:
time: 44.7 us; the launch traced here: 44.6 us
  Pallas kernels  43.9 us (98%)
  between operations  0.64 us (1%)
    pallas_call x1, Pallas kernels, fused(): pl.pallas_call(functools.partial(fused_kernel, n), out_shape=(jax.ShapeDt...  41.6 us
    pallas_call x1, Pallas kernels, turn(): pl.pallas_call(turn_kernel, out_shape=(fresh, jax.ShapeDtypeStruct(curren...  2.3 us

profile of v4, /device:TPU:0, one launch (start us, length us, event | category | flops | bytes accessed | tf_op | source)
XLA Modules:
  0.0 44.6 jit_solution(1327779752192289699)
XLA Ops:
  0.6 41.6 %shard_map.140 = (bf16[2,16,48,256]{3,2,1,0:T(8,128)(2,1)}, f32[2,1,512]{2,1,0:T(1,128)}) custom-call(bf16[48,16,512]{2,1,0:T(8,128)(2,1)} %spectrum_hbm.1, s32[16,512]{1,0:T(8,128)} %mask_hbm.1, s32[16,512]{1,0:T(8,128)} %class_hbm.1, s32[2,768]{1,0:T(2,128)} %signs_hbm.1, f32[8,24]{1,0:T(8,128)} %speed_hbm.1, f32[8,24]{1,0:T(8,128)} %ratio_hbm.1, ...), custom_call_target="tpu_custom_call" | custom-call | tf_op jit(solution)/shard_map/pallas_call | solution.py:673
  42.3 2.3 %shard_map.141 = (bf16[48,16,512]{2,1,0:T(8,128)(2,1)}, f32[2,1,512]{2,1,0:T(1,128)}) custom-call(bf16[2,16,48,256]{3,2,1,0:T(8,128)(2,1)} %get-tuple-element.4.back, f32[2,1,512]{2,1,0:T(1,128)} %get-tuple-element.5.currents_in), custom_call_target="tpu_custom_call" | custom-call | tf_op jit(solution)/shard_map/pallas_call | solution.py:774
